TPU v7x, 512 devices: a whole 4x4x16 slice. The times are simulated.
512 devices in a mesh: row: 16 (over z), col: 32 (over y, x, core).
Axes of the slice: x: 4, y: 4, z: 16, core: 2. Of those that a mesh axis runs over, the one named last changes fastest.
Arguments:
- inputs: bfloat16 [768, 12288], P('col', 'row'), may hold values from -40 to 40
- ln_gain: float32 [12288], P('row'), may hold values from 0.25 to 1.75
- ln_bias: float32 [12288], P('row'), may hold values from -4 to 4
- w_up: bfloat16 [12288, 49152], P('row', 'col'), may hold values from -0.0546875 to 0.0546875
- up_bias: float32 [49152], P('col'), may hold values from -4 to 4
- w_down: bfloat16 [49152, 12288], P('col', 'row'), may hold values from -0.02734375 to 0.02734375
- down_bias: float32 [12288], P('row'), may hold values from -4 to 4
Outputs:
- block_out: bfloat16 [768, 12288], P('col', 'row')
All inputs are finite; a program needn't handle non-finite values.
Results may differ from a plain program's by a relative error of at most 0.0085.
Values may be sent and summed in bfloat16 or wider, within the bound.
A program may use at most 64 MiB of HBM per device.

v0:
```python
import jax
import jax.numpy as jnp
from jax import lax
from jax.sharding import PartitionSpec as P

D = 12288


def local(inputs, ln_gain, ln_bias, w_up, up_bias, w_down, down_bias):
    in_float = inputs.astype(jnp.float32)
    total = lax.psum(jnp.sum(in_float, axis=1), "row")
    average = total / D
    centered = in_float - average[:, None]
    spread = lax.psum(jnp.sum(centered * centered, axis=1), "row")
    variance = spread / D
    normed = (centered * lax.rsqrt(variance + 1e-05)[:, None] * ln_gain + ln_bias).astype(
        jnp.bfloat16
    )
    gathered = lax.all_gather(normed, "col", axis=0, tiled=True)
    summed = lax.psum_scatter(
        jnp.dot(gathered, w_up, preferred_element_type=jnp.float32).astype(jnp.bfloat16),
        "row",
        scatter_dimension=0,
        tiled=True,
    ).astype(jnp.float32)
    hidden = jax.nn.gelu(summed + up_bias, approximate=True).astype(jnp.bfloat16)
    terms = jnp.dot(
        lax.all_gather(hidden, "row", axis=0, tiled=True),
        w_down,
        preferred_element_type=jnp.float32,
    )
    down_sum = lax.psum_scatter(
        terms.astype(jnp.bfloat16), "col", scatter_dimension=0, tiled=True
    ).astype(jnp.float32)
    return (in_float + down_sum + down_bias).astype(jnp.bfloat16)


def solution(mesh):
    placed = (
        P("col", "row"),
        P("row"),
        P("row"),
        P("row", "col"),
        P("col"),
        P("col", "row"),
        P("row"),
    )
    return jax.shard_map(
        local, mesh=mesh, in_specs=placed, out_specs=P("col", "row"), check_vma=False
    )
```

profile of v0, /device:TPU:2, one launch (start us, length us, event | category | flops | bytes accessed | tf_op | source)
XLA Modules:
  0.0 390.2 jit_solution(8472920669554600024)
XLA Ops:
  6.5 0.0 copy-start
  6.5 0.0 all-gather.3.cloned.1.call-start
  6.5 1.0 convert_reduce_fusion
  7.6 36.5 %psum.14 = f32[24]{0:T(128)S(1)} all-reduce(f32[24]{0:T(128)S(1)} %convert_reduce_fusion), channel_id=1, replica_groups=mesh['row'=16,'col'=32] {'row'}, use_global_device_ids=true, to_apply=%region_1.0 | all-reduce | flops 24 | bytes 192 | tf_op jit(solution)/shard_map/psum | solution.py:11
  44.1 1.0 fusion.10
  45.0 27.0 %psum.15 = f32[24]{0:T(128)S(1)} all-reduce(f32[24]{0:T(128)S(1)} %fusion.10), channel_id=1, replica_groups=mesh['row'=16,'col'=32] {'row'}, use_global_device_ids=true, to_apply=%region_3.0 | all-reduce | flops 24 | bytes 192 | tf_op jit(solution)/shard_map/psum | solution.py:14
  72.1 1.5 fusion.13
  73.6 0.0 all-gather.3.cloned.1.call-update
  73.6 0.0 reduce-scatter.3.cloned.1.call-start
  73.6 55.0 %all-gather.3.cloned.1.call-done = bf16[768,768]{1,0:T(8,128)(2,1)} async-done(((bf16[24,768]{1,0:T(8,128)(2,1)}), bf16[768,768]{1,0:T(8,128)(2,1)}) %all-gather.3.cloned.1.call-update) | async-done | bytes 1179664 | tf_op jit(solution)/shard_map/all_gather | solution.py:19
  128.7 0.0 copy-done
  128.7 4.7 %convolution_convert_fusion = bf16[768,1536]{1,0:T(8,128)(2,1)} fusion(bf16[768,768]{1,0:T(8,128)(2,1)} %all-gather.3.cloned.1.call-done, bf16[768,1536]{1,0:T(8,128)(2,1)S(1)} %copy-done), kind=kOutput, calls=%fused_computation | convolution fusion | flops 1813118976 | bytes 5898240 | tf_op jit(solution)/shard_map/dot_general | solution.py:21
  133.3 0.0 copy-start.2
  133.3 0.0 reduce-scatter.3.cloned.1.call-update
  133.4 0.0 all-gather.5.cloned.1.call-start
  133.4 73.7 %reduce-scatter.3.cloned.1.call-done = bf16[48,1536]{1,0:T(8,128)(2,1)} async-done(((bf16[768,1536]{1,0:T(8,128)(2,1)}), bf16[48,1536]{1,0:T(8,128)(2,1)}) %reduce-scatter.3.cloned.1.call-update) | async-done | bytes 147472 | tf_op jit(solution)/shard_map/reduce_scatter | solution.py:20
  207.1 0.0 copy-done.2
  207.1 1.7 fusion.7
  208.8 0.0 all-gather.5.cloned.1.call-update
  208.8 0.0 copy-start.1
  208.8 0.0 copy-start.3
  208.8 0.0 reduce-scatter.5.cloned.1.call-start
  208.9 72.3 %all-gather.5.cloned.1.call-done = bf16[768,1536]{1,0:T(8,128)(2,1)} async-done(((bf16[48,1536]{1,0:T(8,128)(2,1)}), bf16[768,1536]{1,0:T(8,128)(2,1)}) %all-gather.5.cloned.1.call-update) | async-done | bytes 2359312 | tf_op jit(solution)/shard_map/all_gather | solution.py:28
  281.1 5.4 %convolution_convert_fusion.1 = bf16[768,768]{1,0:T(8,128)(2,1)} fusion(bf16[768,1536]{1,0:T(8,128)(2,1)} %all-gather.5.cloned.1.call-done, bf16[1536,768]{1,0:T(8,128)(2,1)} %param.12), kind=kOutput, calls=%fused_computation.1 | convolution fusion | flops 1812529152 | bytes 5898240 | tf_op jit(solution)/shard_map/dot_general | solution.py:27
  286.5 0.0 reduce-scatter.5.cloned.1.call-update
  286.5 95.7 %reduce-scatter.5.cloned.1.call-done = bf16[24,768]{1,0:T(8,128)(2,1)} async-done(((bf16[768,768]{1,0:T(8,128)(2,1)}), bf16[24,768]{1,0:T(8,128)(2,1)}) %reduce-scatter.5.cloned.1.call-update) | async-done | bytes 36880 | tf_op jit(solution)/shard_map/reduce_scatter | solution.py:32
  382.3 0.0 copy-done.1
  382.3 0.0 copy-done.3
  382.3 1.4 fusion.15
  (2 shorter events, 0.0 us)
Async XLA Ops:
  6.5 122.1 %copy-start = (bf16[768,1536]{1,0:T(8,128)(2,1)S(1)}, bf16[768,1536]{1,0:T(8,128)(2,1)}, u32[]{:S(2)}) copy-start(bf16[768,1536]{1,0:T(8,128)(2,1)} %param.10) | copy-start | bytes 7077892
  6.5 122.1 %all-gather.3.cloned.1.call-start = ((), (), s32[]{:S(2)}) async-start(), calls=%async_computation.2 | async-start | bytes 1216512 | tf_op jit(solution)/shard_map/all_gather | solution.py:19
  73.6 133.5 %reduce-scatter.3.cloned.1.call-start = ((), (), s32[]{:S(2)}) async-start(), calls=%async_computation.3 | async-start | bytes 2506752 | tf_op jit(solution)/shard_map/reduce_scatter | solution.py:20
  133.3 73.8 %copy-start.2 = (f32[1536]{0:T(1024)S(1)}, f32[1536]{0:T(1024)}, u32[]{:S(2)}) copy-start(f32[1536]{0:T(1024)} %param.11) | copy-start | bytes 18436
  133.4 147.8 %all-gather.5.cloned.1.call-start = ((), (), s32[]{:S(2)}) async-start(), calls=%async_computation.4 | async-start | bytes 2506752 | tf_op jit(solution)/shard_map/all_gather | solution.py:28
  208.8 173.5 %copy-start.1 = (bf16[24,768]{1,0:T(8,128)(2,1)S(1)}, bf16[24,768]{1,0:T(8,128)(2,1)}, u32[]{:S(2)}) copy-start(bf16[24,768]{1,0:T(8,128)(2,1)} %param.7) | copy-start | bytes 110596
  208.8 173.5 %copy-start.3 = (f32[768]{0:T(1024)S(1)}, f32[768]{0:T(1024)}, u32[]{:S(2)}) copy-start(f32[768]{0:T(1024)} %param.13) | copy-start | bytes 9220
  208.8 173.4 %reduce-scatter.5.cloned.1.call-start = ((), (), s32[]{:S(2)}) async-start(), calls=%async_computation.5 | async-start | bytes 1216512 | tf_op jit(solution)/shard_map/reduce_scatter | solution.py:32
Sparse Core Ops, SparseCore 0:
  73.7 54.8 all-gather.2
  133.5 73.5 reduce-scatter.2
  209.2 71.9 all-gather.4
  286.7 95.5 reduce-scatter.4
where the time goes:
time: 391 us; the launch traced here: 390 us
  waiting for transfers between devices  297 us (76%)
  blocking collectives  63.5 us (16%)
  between operations  13.1 us (3%)
  matrix products  10.1 us (3%)
  other arithmetic  6.57 us (2%)
    reduce_scatter x1, waiting for transfers between devices, local(): lax.psum_scatter(terms.astype(jnp.bfloat16), 'col', scatter_dimension=0,...  95.7 us
    reduce_scatter x1, waiting for transfers between devices, local(): lax.psum_scatter(jnp.dot(gathered, w_up, preferred_element_type=jnp.float...  73.7 us
    all_gather x1, waiting for transfers between devices, local(): lax.all_gather(hidden, 'row', axis=0, tiled=True)  72.3 us
    all_gather x1, waiting for transfers between devices, local(): gathered = lax.all_gather(normed, 'col', axis=0, tiled=True)  55 us
    psum x1, blocking collectives, local(): total = lax.psum(jnp.sum(in_float, axis=1), 'row')  36.5 us
    psum x1, blocking collectives, local(): spread = lax.psum(jnp.sum(centered * centered, axis=1), 'row')  27 us
  transfers between devices with their start and end apart: 4, of which 4 were waited for; matrix products, arithmetic and copies ran while one was open for 0% of the time, Pallas kernels for 0%

commit v1 on v0

--- a/solution.py
+++ b/solution.py
@@ -16,7 +16,9 @@
     normed = (centered * lax.rsqrt(variance + 1e-05)[:, None] * ln_gain + ln_bias).astype(
         jnp.bfloat16
     )
-    gathered = lax.all_gather(normed, "col", axis=0, tiled=True)
+    gathered = jnp.concatenate(
+        lax.all_to_all(jnp.stack([normed] * lax.axis_size("col")), "col", 0, 0), axis=0
+    )
     summed = lax.psum_scatter(
         jnp.dot(gathered, w_up, preferred_element_type=jnp.float32).astype(jnp.bfloat16),
         "row",

time: 391 us -> 354 us (0.905)
  waiting for transfers between devices: 297 us -> 236 us
  blocking collectives: 63.5 us -> 88.8 us
    all_gather x1 -> x0, waiting for transfers between devices: 55 us -> none  [local(): gathered = lax.all_gather(normed, 'col', axis=0, tiled=True)]
    all_to_all x0 -> x1, blocking collectives: none -> 25.3 us  [local(): lax.all_to_all(jnp.stack([normed] * lax.axis_size('col')), 'col', 0, 0)]
    reduce_scatter x1, waiting for transfers between devices: 73.7 us -> 68 us  [local(): lax.psum_scatter(jnp.dot(gathered, w_up, preferred_element_type=jnp.float...]
  transfers between devices with their start and end apart: 4 -> 3, of which waited for: 4 -> 3; matrix products, arithmetic and copies ran while one was open for 0% -> 0% of each run, Pallas kernels for 0% -> 0%
where the time goes in v1:
time: 354 us; the launch traced here: 353 us
  waiting for transfers between devices  236 us (67%)
  blocking collectives  88.8 us (25%)
  between operations  13.1 us (4%)
  matrix products  8.78 us (2%)
  other arithmetic  5.96 us (2%)
    reduce_scatter x1, waiting for transfers between devices, local(): lax.psum_scatter(terms.astype(jnp.bfloat16), 'col', scatter_dimension=0,...  95.8 us
    all_gather x1, waiting for transfers between devices, local(): lax.all_gather(hidden, 'row', axis=0, tiled=True)  72.4 us
    reduce_scatter x1, waiting for transfers between devices, local(): lax.psum_scatter(jnp.dot(gathered, w_up, preferred_element_type=jnp.float...  68 us
    psum x1, blocking collectives, local(): total = lax.psum(jnp.sum(in_float, axis=1), 'row')  36.5 us
    psum x1, blocking collectives, local(): spread = lax.psum(jnp.sum(centered * centered, axis=1), 'row')  27 us
    all_to_all x1, blocking collectives, local(): lax.all_to_all(jnp.stack([normed] * lax.axis_size('col')), 'col', 0, 0)  25.3 us
  transfers between devices with their start and end apart: 3, of which 3 were waited for; matrix products, arithmetic and copies ran while one was open for 0% of the time, Pallas kernels for 0%

profile of v1, /device:TPU:2, one launch (start us, length us, event | category | flops | bytes accessed | tf_op | source)
XLA Modules:
  0.0 353.1 jit_solution(11932974096498430015)
XLA Ops:
  6.5 0.0 copy-start
  6.5 0.0 reduce-scatter.3.cloned.1.call-start
  6.5 1.0 convert_reduce_fusion
  7.6 36.5 %psum.14 = f32[24]{0:T(128)S(1)} all-reduce(f32[24]{0:T(128)S(1)} %convert_reduce_fusion), channel_id=1, replica_groups=mesh['row'=16,'col'=32] {'row'}, use_global_device_ids=true, to_apply=%region_1.0 | all-reduce | flops 24 | bytes 192 | tf_op jit(solution)/shard_map/psum | solution.py:11
  44.1 1.0 fusion.10
  45.0 27.0 %psum.15 = f32[24]{0:T(128)S(1)} all-reduce(f32[24]{0:T(128)S(1)} %fusion.10), channel_id=1, replica_groups=mesh['row'=16,'col'=32] {'row'}, use_global_device_ids=true, to_apply=%region_3.0 | all-reduce | flops 24 | bytes 192 | tf_op jit(solution)/shard_map/psum | solution.py:14
  72.1 0.9 fusion.13
  73.0 0.1 stack.2
  73.0 25.3 %all_to_all.5 = bf16[32,24,768]{2,1,0:T(8,128)(2,1)S(1)} all-to-all(bf16[32,24,768]{2,1,0:T(8,128)(2,1)S(1)} %stack.2), channel_id=1, replica_groups=mesh['row'=16,'col'=32] {'col'}, dimensions={0} | all-to-all | bytes 2359296 | tf_op jit(solution)/shard_map/all_to_all | solution.py:20
  98.3 0.0 copy-done
  98.3 3.4 convolution_convert_fusion
  101.7 0.0 copy-start.2
  101.7 0.0 reduce-scatter.3.cloned.1.call-update
  101.7 0.0 all-gather.2.cloned.1.call-start
  101.8 68.0 %reduce-scatter.3.cloned.1.call-done = bf16[48,1536]{1,0:T(8,128)(2,1)} async-done(((bf16[768,1536]{1,0:T(8,128)(2,1)}), bf16[48,1536]{1,0:T(8,128)(2,1)}) %reduce-scatter.3.cloned.1.call-update) | async-done | bytes 147472 | tf_op jit(solution)/shard_map/reduce_scatter | solution.py:22
  169.8 0.0 copy-done.2
  169.8 1.7 fusion.7
  171.5 0.0 all-gather.2.cloned.1.call-update
  171.5 0.0 copy-start.1
  171.5 0.0 copy-start.3
  171.6 0.0 reduce-scatter.5.cloned.1.call-start
  171.6 72.4 %all-gather.2.cloned.1.call-done = bf16[768,1536]{1,0:T(8,128)(2,1)} async-done(((bf16[48,1536]{1,0:T(8,128)(2,1)}), bf16[768,1536]{1,0:T(8,128)(2,1)}) %all-gather.2.cloned.1.call-update) | async-done | bytes 2359312 | tf_op jit(solution)/shard_map/all_gather | solution.py:30
  244.0 5.4 %convolution_convert_fusion.1 = bf16[768,768]{1,0:T(8,128)(2,1)} fusion(bf16[768,1536]{1,0:T(8,128)(2,1)} %all-gather.2.cloned.1.call-done, bf16[1536,768]{1,0:T(8,128)(2,1)} %param.12), kind=kOutput, calls=%fused_computation.1 | convolution fusion | flops 1812529152 | bytes 5898240 | tf_op jit(solution)/shard_map/dot_general | solution.py:29
  249.4 0.0 reduce-scatter.5.cloned.1.call-update
  249.4 95.8 %reduce-scatter.5.cloned.1.call-done = bf16[24,768]{1,0:T(8,128)(2,1)} async-done(((bf16[768,768]{1,0:T(8,128)(2,1)}), bf16[24,768]{1,0:T(8,128)(2,1)}) %reduce-scatter.5.cloned.1.call-update) | async-done | bytes 36880 | tf_op jit(solution)/shard_map/reduce_scatter | solution.py:34
  345.2 0.0 copy-done.1
  345.2 0.0 copy-done.3
  345.2 1.4 fusion.15
  (2 shorter events, 0.0 us)
Async XLA Ops:
  6.5 91.8 %copy-start = (bf16[768,1536]{1,0:T(8,128)(2,1)S(1)}, bf16[768,1536]{1,0:T(8,128)(2,1)}, u32[]{:S(2)}) copy-start(bf16[768,1536]{1,0:T(8,128)(2,1)} %param.10) | copy-start | bytes 7077892
  6.5 163.3 %reduce-scatter.3.cloned.1.call-start = ((), (), s32[]{:S(2)}) async-start(), calls=%async_computation.3 | async-start | bytes 2506752 | tf_op jit(solution)/shard_map/reduce_scatter | solution.py:22
  101.7 68.1 %copy-start.2 = (f32[1536]{0:T(1024)S(1)}, f32[1536]{0:T(1024)}, u32[]{:S(2)}) copy-start(f32[1536]{0:T(1024)} %param.11) | copy-start | bytes 18436
  101.7 142.3 %all-gather.2.cloned.1.call-start = ((), (), s32[]{:S(2)}) async-start(), calls=%async_computation.4 | async-start | bytes 2506752 | tf_op jit(solution)/shard_map/all_gather | solution.py:30
  171.5 173.6 %copy-start.1 = (bf16[24,768]{1,0:T(8,128)(2,1)S(1)}, bf16[24,768]{1,0:T(8,128)(2,1)}, u32[]{:S(2)}) copy-start(bf16[24,768]{1,0:T(8,128)(2,1)} %param.7) | copy-start | bytes 110596
  171.5 173.6 %copy-start.3 = (f32[768]{0:T(1024)S(1)}, f32[768]{0:T(1024)}, u32[]{:S(2)}) copy-start(f32[768]{0:T(1024)} %param.13) | copy-start | bytes 9220
  171.6 173.6 %reduce-scatter.5.cloned.1.call-start = ((), (), s32[]{:S(2)}) async-start(), calls=%async_computation.5 | async-start | bytes 1216512 | tf_op jit(solution)/shard_map/reduce_scatter | solution.py:34
Sparse Core Ops, SparseCore 0:
  101.9 67.9 reduce-scatter.2
  171.9 72.0 all-gather.1
  249.5 95.5 reduce-scatter.4
